TPU v7x, 512 devices: a whole 4x8x8 slice. The times are simulated.
512 devices in a mesh: chan: 8 (over x, core), tm: 64 (over z, y).
Axes of the slice: x: 4, y: 8, z: 8, core: 2. Of those that a mesh axis runs over, the one named last changes fastest.
Arguments:
- traces: float32 [64, 512, 6144], P('tm', 'chan')
- channel_map: int32 [512], P('chan'), may hold values from 0 to 511, as said below
- pair_blocks: int32 [32, 2], replicated, may hold values from 0 to 31, as said below
- pair_count: int32 [8], replicated, may hold values from 1 to 1024, as said below
Outputs:
- correlations: float32 [8192, 4096], P(('chan', 'tm'))
Inputs may be any that keep to these rules, and one draw needn't show every extreme that they name: `channel_map`: entries 64 * d to 64 * d + 63 are an ordering of those same numbers. `pair_blocks`: in every row the first block is at most the second, and the second at most the first plus 4. `pair_count`: some owner has all its pairs live.
All inputs are finite; a program needn't handle non-finite values.
Results may differ from a plain program's by a relative error of at most 0.0017.
Values may be sent and summed in bfloat16 or wider, within the bound.
A program may use at most 64 MiB of HBM per device.

v0:
```python
import math

import jax
import jax.numpy as jnp
from jax import lax
from jax.sharding import PartitionSpec as P

BLOCK_CHANNELS = 16
OWNER_SLOTS = 4
TRANSFORM_LENGTH = 16384
BAND_FIRST_BIN = 80
BAND_BINS = 512
LAGS = 4096


def forward_spectrum(minute_window):
    chan_rows, samples = minute_window.shape
    block_len = 512
    frequency_indices = BAND_FIRST_BIN + jnp.arange(BAND_BINS, dtype=jnp.int32)

    def add_block(block_idx, running):
        begin_at = block_idx * block_len
        trace_part = lax.dynamic_slice_in_dim(minute_window, begin_at, block_len, 1)
        sample_ids = begin_at + jnp.arange(block_len, dtype=jnp.int32)
        angles = jnp.mod(sample_ids[:, None] * frequency_indices[None, :], TRANSFORM_LENGTH).astype(
            jnp.float32
        ) * (2.0 * math.pi / TRANSFORM_LENGTH)
        basis_rows = jnp.concatenate([jnp.cos(angles), -jnp.sin(angles)], axis=1)
        return running + jnp.dot(
            trace_part,
            basis_rows,
            precision=lax.Precision.HIGHEST,
            preferred_element_type=jnp.float32,
        )

    return lax.fori_loop(
        0, samples // block_len, add_block, jnp.zeros((chan_rows, 2 * BAND_BINS), jnp.float32)
    )


def whiten(window_spectrum):
    real_part = window_spectrum[:, :BAND_BINS]
    imag_part = window_spectrum[:, BAND_BINS:]
    power = real_part * real_part + imag_part * imag_part
    band_level = jnp.mean(power, axis=1, keepdims=True)
    inverse = 1.0 / jnp.sqrt(power + band_level + 1e-06)
    return jnp.concatenate([real_part * inverse, imag_part * inverse], axis=1).astype(jnp.bfloat16)


def inverse_transform(stacked):
    lag_block = 1024
    frequency_indices = BAND_FIRST_BIN + jnp.arange(BAND_BINS, dtype=jnp.int32)
    results = []
    for block_idx in range(LAGS // lag_block):
        lag_ids = block_idx * lag_block + jnp.arange(lag_block, dtype=jnp.int32) - LAGS // 2
        angles = jnp.mod(frequency_indices[:, None] * lag_ids[None, :], TRANSFORM_LENGTH).astype(
            jnp.float32
        ) * (2.0 * math.pi / TRANSFORM_LENGTH)
        basis_rows = jnp.concatenate([jnp.cos(angles), -jnp.sin(angles)], axis=0)
        results.append(
            jnp.dot(
                stacked,
                basis_rows,
                precision=lax.Precision.HIGHEST,
                preferred_element_type=jnp.float32,
            )
        )
    return jnp.concatenate(results, axis=1) * (1.0 / math.sqrt(BAND_BINS))


def body(traces, channel_map, pair_blocks, pair_count):
    chan_dev = traces.shape[1]
    whitened = whiten(forward_spectrum(traces[0]))
    fibre_rows = jnp.take(whitened, jnp.mod(channel_map, chan_dev), axis=0)
    all_blocks = lax.all_gather(fibre_rows, "chan", axis=0, tiled=True)
    owner_idx = lax.axis_index("chan")
    owned_pairs = lax.dynamic_slice_in_dim(pair_blocks, owner_idx * OWNER_SLOTS, OWNER_SLOTS, 0)
    offsets = jnp.arange(BLOCK_CHANNELS, dtype=jnp.int32)
    block_first = jnp.take(
        all_blocks, (owned_pairs[:, 0:1] * BLOCK_CHANNELS + offsets[None, :]).reshape(-1), axis=0
    )
    block_second = jnp.take(
        all_blocks, (owned_pairs[:, 1:2] * BLOCK_CHANNELS + offsets[None, :]).reshape(-1), axis=0
    )
    windows = lax.axis_size("tm")
    pair_rows = OWNER_SLOTS * BLOCK_CHANNELS * BLOCK_CHANNELS
    row_share = pair_rows // windows
    row_ids = jnp.arange(lax.axis_size("tm") * row_share, dtype=jnp.int32)
    left_rows = jnp.take(block_first, row_ids // BLOCK_CHANNELS, axis=0).astype(jnp.float32)
    right_rows = jnp.take(
        block_second,
        row_ids // (BLOCK_CHANNELS * BLOCK_CHANNELS) * BLOCK_CHANNELS
        + jnp.mod(row_ids, BLOCK_CHANNELS),
        axis=0,
    ).astype(jnp.float32)
    left_re = left_rows[:, :BAND_BINS]
    left_im = left_rows[:, BAND_BINS:]
    right_re = right_rows[:, :BAND_BINS]
    right_im = right_rows[:, BAND_BINS:]
    stacked = lax.psum_scatter(
        jnp.concatenate(
            [left_re * right_re + left_im * right_im, left_im * right_re - left_re * right_im],
            axis=1,
        ),
        "tm",
        scatter_dimension=0,
        tiled=True,
    )
    stacked = stacked * (1.0 / math.sqrt(windows))
    row_ids = lax.axis_index("tm") * row_share + jnp.arange(row_share, dtype=jnp.int32)
    live_count = lax.dynamic_slice_in_dim(pair_count, owner_idx, 1, 0)
    live_mask = (row_ids < live_count).astype(jnp.float32)
    return inverse_transform(stacked) * live_mask[:, None]


def solution(mesh):
    placed = (P("tm", "chan", None), P("chan"), P(), P())
    return jax.shard_map(
        body, mesh=mesh, in_specs=placed, out_specs=P(("chan", "tm"), None), check_vma=False
    )
```

profile of v0, /device:TPU:1, one launch (start us, length us, event | category | flops | bytes accessed | tf_op | source)
XLA Modules:
  0.0 401.1 jit_solution(11808629027902082679)
XLA Ops:
  7.2 78.5 %while.16 = (s32[]{:T(128)}, f32[64,1024]{1,0:T(8,128)S(1)}, f32[64,6144]{1,0:T(8,128)}, s32[]{:T(128)}, s32[]{:T(128)}, /*index=5*/s32[]{:T(128)}, s32[]{:T(128)}) while((s32[]{:T(128)}, f32[64,1024]{1,0:T(8,128)S(1)}, f32[64,6144]{1,0:T(8,128)}, s32[]{:T(128)}, s32[]{:T(128)}, /*index=5*/s32[]{:T(128)}, s32[]{:T(128)}) %tuple.70), condition=%wide.region_1.2_spmd.clone, body=%wide.region_0.1_spmd.clone.sunk | while | flops 407241728 | bytes 4858005 | solution.py:36
  7.3 4.2 %fusion.90 = (f32[512,512]{1,0:T(8,128)S(1)}, f32[512,512]{1,0:T(8,128)S(1)}) fusion(s32[512]{0:T(512)S(1)} %get-tuple-element.190, s32[512]{0:T(512)S(1)} %get-tuple-element.191), kind=kLoop, calls=%fused_computation.20.clone.1 | loop fusion | flops 3932160 | bytes 2101248 | tf_op jit(solution)/shard_map/while/body/eval_jaxpr/cos | solution.py:28
  13.8 4.2 %fusion.90 = (f32[512,512]{1,0:T(8,128)S(1)}, f32[512,512]{1,0:T(8,128)S(1)}) fusion(s32[512]{0:T(512)S(1)} %get-tuple-element.190, s32[512]{0:T(512)S(1)} %get-tuple-element.191), kind=kLoop, calls=%fused_computation.20.clone.1 | loop fusion | flops 3932160 | bytes 2101248 | tf_op jit(solution)/shard_map/while/body/eval_jaxpr/cos | solution.py:28
  18.0 2.3 fusion.91
  20.4 4.2 %fusion.90 = (f32[512,512]{1,0:T(8,128)S(1)}, f32[512,512]{1,0:T(8,128)S(1)}) fusion(s32[512]{0:T(512)S(1)} %get-tuple-element.190, s32[512]{0:T(512)S(1)} %get-tuple-element.191), kind=kLoop, calls=%fused_computation.20.clone.1 | loop fusion | flops 3932160 | bytes 2101248 | tf_op jit(solution)/shard_map/while/body/eval_jaxpr/cos | solution.py:28
  26.9 4.2 %fusion.90 = (f32[512,512]{1,0:T(8,128)S(1)}, f32[512,512]{1,0:T(8,128)S(1)}) fusion(s32[512]{0:T(512)S(1)} %get-tuple-element.190, s32[512]{0:T(512)S(1)} %get-tuple-element.191), kind=kLoop, calls=%fused_computation.20.clone.1 | loop fusion | flops 3932160 | bytes 2101248 | tf_op jit(solution)/shard_map/while/body/eval_jaxpr/cos | solution.py:28
  31.1 2.3 fusion.91
  33.4 4.2 %fusion.90 = (f32[512,512]{1,0:T(8,128)S(1)}, f32[512,512]{1,0:T(8,128)S(1)}) fusion(s32[512]{0:T(512)S(1)} %get-tuple-element.190, s32[512]{0:T(512)S(1)} %get-tuple-element.191), kind=kLoop, calls=%fused_computation.20.clone.1 | loop fusion | flops 3932160 | bytes 2101248 | tf_op jit(solution)/shard_map/while/body/eval_jaxpr/cos | solution.py:28
  40.0 4.2 %fusion.90 = (f32[512,512]{1,0:T(8,128)S(1)}, f32[512,512]{1,0:T(8,128)S(1)}) fusion(s32[512]{0:T(512)S(1)} %get-tuple-element.190, s32[512]{0:T(512)S(1)} %get-tuple-element.191), kind=kLoop, calls=%fused_computation.20.clone.1 | loop fusion | flops 3932160 | bytes 2101248 | tf_op jit(solution)/shard_map/while/body/eval_jaxpr/cos | solution.py:28
  44.2 2.3 fusion.91
  46.5 4.2 %fusion.90 = (f32[512,512]{1,0:T(8,128)S(1)}, f32[512,512]{1,0:T(8,128)S(1)}) fusion(s32[512]{0:T(512)S(1)} %get-tuple-element.190, s32[512]{0:T(512)S(1)} %get-tuple-element.191), kind=kLoop, calls=%fused_computation.20.clone.1 | loop fusion | flops 3932160 | bytes 2101248 | tf_op jit(solution)/shard_map/while/body/eval_jaxpr/cos | solution.py:28
  53.1 4.2 %fusion.90 = (f32[512,512]{1,0:T(8,128)S(1)}, f32[512,512]{1,0:T(8,128)S(1)}) fusion(s32[512]{0:T(512)S(1)} %get-tuple-element.190, s32[512]{0:T(512)S(1)} %get-tuple-element.191), kind=kLoop, calls=%fused_computation.20.clone.1 | loop fusion | flops 3932160 | bytes 2101248 | tf_op jit(solution)/shard_map/while/body/eval_jaxpr/cos | solution.py:28
  57.3 2.3 fusion.91
  59.6 4.2 %fusion.90 = (f32[512,512]{1,0:T(8,128)S(1)}, f32[512,512]{1,0:T(8,128)S(1)}) fusion(s32[512]{0:T(512)S(1)} %get-tuple-element.190, s32[512]{0:T(512)S(1)} %get-tuple-element.191), kind=kLoop, calls=%fused_computation.20.clone.1 | loop fusion | flops 3932160 | bytes 2101248 | tf_op jit(solution)/shard_map/while/body/eval_jaxpr/cos | solution.py:28
  66.2 4.2 %fusion.90 = (f32[512,512]{1,0:T(8,128)S(1)}, f32[512,512]{1,0:T(8,128)S(1)}) fusion(s32[512]{0:T(512)S(1)} %get-tuple-element.190, s32[512]{0:T(512)S(1)} %get-tuple-element.191), kind=kLoop, calls=%fused_computation.20.clone.1 | loop fusion | flops 3932160 | bytes 2101248 | tf_op jit(solution)/shard_map/while/body/eval_jaxpr/cos | solution.py:28
  72.7 4.2 %fusion.90 = (f32[512,512]{1,0:T(8,128)S(1)}, f32[512,512]{1,0:T(8,128)S(1)}) fusion(s32[512]{0:T(512)S(1)} %get-tuple-element.190, s32[512]{0:T(512)S(1)} %get-tuple-element.191), kind=kLoop, calls=%fused_computation.20.clone.1 | loop fusion | flops 3932160 | bytes 2101248 | tf_op jit(solution)/shard_map/while/body/eval_jaxpr/cos | solution.py:28
  79.3 4.2 %fusion.90 = (f32[512,512]{1,0:T(8,128)S(1)}, f32[512,512]{1,0:T(8,128)S(1)}) fusion(s32[512]{0:T(512)S(1)} %get-tuple-element.190, s32[512]{0:T(512)S(1)} %get-tuple-element.191), kind=kLoop, calls=%fused_computation.20.clone.1 | loop fusion | flops 3932160 | bytes 2101248 | tf_op jit(solution)/shard_map/while/body/eval_jaxpr/cos | solution.py:28
  83.5 2.3 fusion.91
  88.2 34.2 %all-gather.2.cloned.1.call-done = bf16[512,1024]{1,0:T(8,128)(2,1)} async-done(((bf16[64,1024]{1,0:T(8,128)(2,1)}), bf16[512,1024]{1,0:T(8,128)(2,1)}) %all-gather.2.cloned.1.call-update) | async-done | bytes 1048592 | tf_op jit(solution)/shard_map/all_gather | solution.py:75
  125.6 4.1 %gather_fusion.4 = bf16[1024,1024]{1,0:T(8,128)(2,1)S(1)} fusion(bf16[64,1024]{1,0:T(8,128)(2,1)S(1)} %broadcast_select_fusion, s32[1024]{0:T(1024)S(1)} %broadcast_clamp_fusion), kind=kCustom, calls=%fused_computation.3.clone | custom fusion | bytes 4198400 | tf_op jit(solution)/shard_map/jit(_take)/gather | solution.py:90
  129.6 5.4 %gather_fusion.2 = bf16[1024,1024]{1,0:T(8,128)(2,1)} fusion(bf16[64,1024]{1,0:T(8,128)(2,1)S(1)} %broadcast_select_fusion.1, s32[1024]{0:T(1024)S(1)} %fusion.70), kind=kCustom, calls=%fused_computation.1.clone | custom fusion | bytes 4198400 | tf_op jit(solution)/shard_map/jit(_take)/gather | solution.py:89
  142.5 36.2 %fusion.50 = (f32[512,1024]{1,0:T(8,128)}, f32[512,1024]{1,0:T(8,128)}, f32[512,1024]{1,0:T(8,128)}, f32[512,1024]{1,0:T(8,128)}, f32[512,1024]{1,0:T(8,128)}, /...) fusion(s32[1024]{0:T(1024)S(1)} %iota_add_fusion.4, s32[512]{0:T(512)S(1)} %iota_add_fusion.7, ...), kind=kLoop, calls=%fused_computation.87 | loop fusion | flops 31457280 | bytes 16791552 | tf_op jit(solution)/shard_map/cos | solution.py:59
  178.7 203.8 %reduce-scatter.2.cloned.1.call-done = f32[16,1024]{1,0:T(8,128)} async-done(((f32[1024,1024]{1,0:T(8,128)}), f32[16,1024]{1,0:T(8,128)}) %reduce-scatter.2.cloned.1.call-update) | async-done | bytes 65552 | tf_op jit(solution)/shard_map/reduce_scatter | solution.py:100
  382.6 4.5 %fusion.16 = f32[16,1024]{1,0:T(8,128)S(1)} fusion(f32[512,1024]{1,0:T(8,128)} %get-tuple-element.150, f32[512,1024]{1,0:T(8,128)} %get-tuple-element.149, f32[16,1024]{1,0:T(8,128)} %reduce-scatter.2.cloned.1.call-done), kind=kOutput, calls=%fused_computation.27 | convolution fusion | flops 202391552 | bytes 4325376 | tf_op jit(solution)/shard_map/dot_general | solution.py:61
  (82 shorter events, 37.0 us)
Async XLA Ops:
  6.5 81.2 %copy-start = (s32[32,2]{0,1:T(2,128)S(1)}, s32[32,2]{0,1:T(2,128)}, u32[]{:S(2)}) copy-start(s32[32,2]{0,1:T(2,128)} %param.12) | copy-start | bytes 772
  6.5 115.9 %all-gather.2.cloned.1.call-start = ((), (), s32[]{:S(2)}) async-start(), calls=%async_computation.1 | async-start | bytes 1179648 | tf_op jit(solution)/shard_map/all_gather | solution.py:75
  87.5 295.1 %reduce-scatter.2.cloned.1.call-start = ((), (), s32[]{:S(2)}) async-start(), calls=%async_computation.2 | async-start | bytes 4259840 | tf_op jit(solution)/shard_map/reduce_scatter | solution.py:100
  122.4 2.3 copy-start.6
  140.6 0.7 copy-start.8
  382.6 4.5 %copy-start.4 = (f32[512,1024]{1,0:T(8,128)S(1)}, f32[512,1024]{1,0:T(8,128)}, u32[]{:S(2)}) copy-start(f32[512,1024]{1,0:T(8,128)} %get-tuple-element.155) | copy-start | bytes 6291460
  382.6 4.5 %copy-start.5 = (f32[512,1024]{1,0:T(8,128)S(1)}, f32[512,1024]{1,0:T(8,128)}, u32[]{:S(2)}) copy-start(f32[512,1024]{1,0:T(8,128)} %get-tuple-element.158) | copy-start | bytes 6291460
  382.6 4.5 %copy-start.7 = (f32[16,1024]{1,0:T(8,128)S(1)}, f32[16,1024]{1,0:T(8,128)}, u32[]{:S(2)}) copy-start(f32[16,1024]{1,0:T(8,128)} %reduce-scatter.2.cloned.1.call-done) | copy-start | bytes 196612
  387.1 2.1 copy-start.2
  387.1 2.2 copy-start.3
  389.3 2.1 copy-start.1
Sparse Core Ops, SparseCore 0:
  87.6 34.7 all-gather.1
  140.7 241.7 reduce-scatter.1
where the time goes:
time: 405 us; the launch traced here: 401 us
  waiting for transfers between devices  238 us (59%)
  other arithmetic  95.5 us (24%)
  matrix products  38.5 us (10%)
  local copies, waits for them, and re-layouts  14.7 us (4%)
  between operations  13.6 us (3%)
    reduce_scatter x1, waiting for transfers between devices, body(): lax.psum_scatter(jnp.concatenate([left_re * right_re + left_im * right_im...  204 us
    cos x12, other arithmetic, add_block(): basis_rows = jnp.concatenate([jnp.cos(angles), -jnp.sin(angles)], axis=1)  50.2 us
    cos x1, other arithmetic, inverse_transform(): basis_rows = jnp.concatenate([jnp.cos(angles), -jnp.sin(angles)], axis=0)  36.2 us
    all_gather x1, waiting for transfers between devices, body(): all_blocks = lax.all_gather(fibre_rows, 'chan', axis=0, tiled=True)  34.2 us
    dot_general x12, matrix products, add_block(): jnp.dot(trace_part, basis_rows, precision=lax.Precision.HIGHEST, preferre...  27.8 us
    dot_general x4, matrix products, inverse_transform(): jnp.dot(stacked, basis_rows, precision=lax.Precision.HIGHEST, preferred_e...  10.8 us
  transfers between devices with their start and end apart: 2, of which 2 were waited for; matrix products, arithmetic and copies ran while one was open for 9% of the time, Pallas kernels for 0%

commit v1 on v0

v1 whole, which is shorter than its diff:
```python
import math

import jax
import jax.numpy as jnp
import numpy as np
from jax import lax
from jax.sharding import PartitionSpec as P

BLOCK_CHANNELS = 16
TRANSFORM_LENGTH = 16384
BAND_FIRST_BIN = 80
BAND_BINS = 512
LAGS = 4096
FIRST = 512
LAG_FIRST = 256
HIGHEST = lax.Precision.HIGHEST


def phase(products):
    angles = np.mod(products, TRANSFORM_LENGTH) * (2.0 * math.pi / TRANSFORM_LENGTH)
    return np.cos(angles).astype(np.float32), np.sin(angles).astype(np.float32)


def forward_spectrum(window):
    rows, samples = window.shape
    bins = BAND_FIRST_BIN + np.arange(BAND_BINS)
    cos_t, sin_t = phase(np.arange(FIRST)[:, None] * bins[None, :])
    cos_w, sin_w = phase(np.arange(samples // FIRST)[:, None] * FIRST * bins[None, :])
    parts = window.reshape(rows, samples // FIRST, FIRST)
    re = jnp.einsum("cba,ak->bck", parts, cos_t, precision=HIGHEST)
    im = jnp.einsum("cba,ak->bck", parts, -sin_t, precision=HIGHEST)
    cos_w, sin_w = cos_w[:, None, :], sin_w[:, None, :]
    return jnp.sum(re * cos_w + im * sin_w, 0), jnp.sum(im * cos_w - re * sin_w, 0)


def whiten(re, im):
    power = re * re + im * im
    level = jnp.mean(power, axis=1, keepdims=True)
    inverse = 1.0 / jnp.sqrt(power + level + 1e-06)
    return (re * inverse).astype(jnp.bfloat16), (im * inverse).astype(jnp.bfloat16)


def inverse_transform(re, im):
    rows = re.shape[0]
    bins = BAND_FIRST_BIN + np.arange(BAND_BINS)
    far = np.arange(LAGS // LAG_FIRST) * LAG_FIRST - LAGS // 2
    cos_w, sin_w = phase(far[:, None, None] * bins[None, None, :])
    cos_t, sin_t = phase(bins[:, None] * np.arange(LAG_FIRST)[None, :])
    table = np.concatenate([cos_t, -sin_t], axis=0)
    turned = jnp.concatenate([re * cos_w - im * sin_w, re * sin_w + im * cos_w], axis=2)
    out = jnp.einsum("nrk,kl->rnl", turned, table, precision=HIGHEST)
    return out.reshape(rows, LAGS) * (1.0 / math.sqrt(BAND_BINS))


def body(traces, channel_map, pair_blocks, pair_count):
    chan_dev = traces.shape[1]
    chans, windows = lax.axis_size("chan"), lax.axis_size("tm")
    re, im = whiten(*forward_spectrum(traces[0]))
    fibre = jnp.stack([re, im], axis=0)
    fibre = jnp.take(fibre, jnp.mod(channel_map, chan_dev), axis=1)
    fibre = jnp.transpose(fibre.reshape(2, chan_dev, windows, chans), (2, 3, 1, 0))
    fibre = lax.all_to_all(fibre, "tm", 0, 0, tiled=True)
    fibre = jnp.transpose(fibre, (1, 2, 0, 3))
    fibre = lax.all_to_all(fibre, "chan", 0, 0, tiled=True)
    blocks = fibre.reshape(-1, BLOCK_CHANNELS, windows, 2).astype(jnp.float32)
    left = jnp.take(blocks, pair_blocks[:, 0], axis=0)
    right = jnp.take(blocks, pair_blocks[:, 1], axis=0)
    swapped = jnp.stack([right[..., 1], -right[..., 0]], axis=-1)
    both = jnp.stack([right, -swapped], axis=1).reshape(right.shape[0], 2, BLOCK_CHANNELS, -1)
    left = left.reshape(left.shape[0], BLOCK_CHANNELS, -1)
    stacked = jnp.einsum("piw,pcjw->pijc", left, both, precision=HIGHEST) * (1.0 / math.sqrt(windows))
    stacked = stacked.reshape(chans, -1, 2)
    stacked = lax.all_to_all(stacked, "chan", 0, 0, tiled=True)
    stacked = jnp.transpose(stacked.reshape(chans, windows, -1, 2), (1, 0, 2, 3))
    stacked = lax.all_to_all(stacked, "tm", 0, 0, tiled=True)
    stacked = jnp.transpose(stacked.reshape(BAND_BINS, -1, 2), (2, 1, 0))
    rows = stacked.shape[1]
    row_ids = lax.axis_index("tm") * rows + jnp.arange(rows, dtype=jnp.int32)
    live = lax.dynamic_slice_in_dim(pair_count, lax.axis_index("chan"), 1, 0)
    mask = (row_ids < live).astype(jnp.float32)
    return inverse_transform(stacked[0], stacked[1]) * mask[:, None]


def solution(mesh):
    placed = (P("tm", "chan", None), P("chan"), P(), P())
    return jax.shard_map(
        body, mesh=mesh, in_specs=placed, out_specs=P(("chan", "tm"), None), check_vma=False
    )
```

time: 405 us -> 90.8 us (0.22)
  waiting for transfers between devices: 238 us -> 26.7 us
  other arithmetic: 95.5 us -> 2.97 us
  matrix products: 38.5 us -> 8.7 us
  starting transfers between devices: 0.22 us -> 28.2 us
  between operations: 13.6 us -> 0.49 us
  blocking collectives: 0 us -> 8.09 us
    reduce_scatter x1 -> x0, waiting for transfers between devices: 204 us -> none  [body(): lax.psum_scatter(jnp.concatenate([left_re * right_re + left_im * right_im...]
    cos x13 -> x0, other arithmetic: 86.4 us -> none  [the longest x12 50.2 us: add_block(): basis_rows = jnp.concatenate([jnp.cos(angles), -jnp.sin(angles)], axis=1)]
    all_gather x1 -> x0, waiting for transfers between devices: 34.2 us -> none  [body(): all_blocks = lax.all_gather(fibre_rows, 'chan', axis=0, tiled=True)]
    dot_general x16 -> x4, matrix products: 38.5 us -> 8.7 us  [the longest x1 3.75 us: forward_spectrum(): im = jnp.einsum('cba,ak->bck', parts, -sin_t, precision=HIGHEST)]
    all_to_all x0 -> x3, starting transfers between devices: none -> 28.2 us  [the longest x1 17.1 us: body(): fibre = lax.all_to_all(fibre, 'tm', 0, 0, tiled=True)]
    all_to_all x0 -> x3, waiting for transfers between devices: none -> 26.7 us  [the longest x1 11.5 us: body(): fibre = lax.all_to_all(fibre, 'tm', 0, 0, tiled=True)]
    gather x5 -> x4, local copies, waits for them, and re-layouts: 13.1 us -> 2.2 us  [the longest x2 1.03 us: body(): fibre = jnp.take(fibre, jnp.mod(channel_map, chan_dev), axis=1)]
    all_to_all x0 -> x1, blocking collectives: none -> 8.09 us  [body(): stacked = lax.all_to_all(stacked, 'chan', 0, 0, tiled=True)]
  transfers between devices with their start and end apart: 2 -> 3, of which waited for: 2 -> 3; matrix products, arithmetic and copies ran while one was open for 9% -> 1% of each run, Pallas kernels for 0% -> 0%
where the time goes in v1:
time: 90.8 us; the launch traced here: 90.4 us
  starting transfers between devices  28.2 us (31%)
  waiting for transfers between devices  26.7 us (29%)
  local copies, waits for them, and re-layouts  15.3 us (17%)
  matrix products  8.7 us (10%)
  blocking collectives  8.09 us (9%)
  other arithmetic  2.97 us (3%)
    all_to_all x1, starting transfers between devices, body(): fibre = lax.all_to_all(fibre, 'tm', 0, 0, tiled=True)  17.1 us
    all_to_all x1, waiting for transfers between devices, body(): fibre = lax.all_to_all(fibre, 'tm', 0, 0, tiled=True)  11.5 us
    all_to_all x1, waiting for transfers between devices, body(): stacked = lax.all_to_all(stacked, 'tm', 0, 0, tiled=True)  9.9 us
    all_to_all x1, blocking collectives, body(): stacked = lax.all_to_all(stacked, 'chan', 0, 0, tiled=True)  8.09 us
    all_to_all x1, starting transfers between devices, body(): fibre = lax.all_to_all(fibre, 'chan', 0, 0, tiled=True)  6.42 us
    all_to_all x1, waiting for transfers between devices, body(): fibre = lax.all_to_all(fibre, 'chan', 0, 0, tiled=True)  5.25 us
    all_to_all x1, starting transfers between devices, body(): stacked = lax.all_to_all(stacked, 'tm', 0, 0, tiled=True)  4.62 us
    unnamed x26, local copies, waits for them, and re-layouts  4.1 us
  transfers between devices with their start and end apart: 3, of which 3 were waited for; matrix products, arithmetic and copies ran while one was open for 1% of the time, Pallas kernels for 0%

profile of v1, /device:TPU:1, one launch (start us, length us, event | category | flops | bytes accessed | tf_op | source)
XLA Modules:
  0.0 90.4 jit_solution(5094060478940147455)
XLA Ops:
  0.0 1.8 %reshape_squeeze.3 = f32[64,12,512]{2,1,0:T(8,128)S(1)} reshape(f32[1,64,6144]{2,1,0:T(8,128)} %param.13) | data formatting | bytes 3145728 | tf_op jit(solution)/shard_map/reshape;squeeze | solution.py:29
  1.9 3.4 %fusion.7 = f32[512,64,12]{0,1,2:T(8,128)S(1)} fusion(f32[512,512,1]{1,0,2:T(8,128)S(1)} %copy-done, f32[64,12,512]{2,1,0:T(8,128)S(1)} %reshape_squeeze.3), kind=kOutput, calls=%fused_computation.15 | convolution fusion | flops 2415919104 | bytes 4194304 | tf_op jit(solution)/shard_map/cba,ak->bck/dot_general | solution.py:30
  5.3 3.8 %fusion.1 = (f32[64,512]{1,0:T(8,128)S(1)}, f32[64,512]{1,0:T(8,128)S(1)}) fusion(f32[512,64,12]{0,1,2:T(8,128)S(1)} %fusion.7, f32[12,512]{1,0:T(8,128)S(1)} %copy-done.9, f32[12,512]{1,0:T(8,128)S(1)} %copy-done.8, f32[512,512,1]{1,0,2:T(8,128)S(1)} %copy-done.7, f32[64,12,512]{2,1,0:T(8,128)S(1)} %reshape_squeeze.3), kind=kOutput, calls=%fused_computation.6 | convolution fusion | flops 2418999296 | bytes 4505600 | tf_op jit(solution)/shard_map/cba,ak->bck/dot_general | solution.py:31
  9.5 0.8 gather_fusion
  10.6 0.8 reshape.182
  11.5 17.1 %all-to-all-start = ((bf16[64,2,512]{2,1,0:T(2,128)(2,1)}), bf16[64,2,512]{2,1,0:T(2,128)(2,1)S(1)}, u32[]{:S(2)}, u32[]{:S(2)}) async-start(bf16[64,2,512]{2,1,0:T(2,128)(2,1)} %reshape.182), calls=%async_computation | async-start | bytes 262144 | tf_op jit(solution)/shard_map/all_to_all | solution.py:62
  28.6 11.5 %all-to-all-done = bf16[64,2,512]{2,1,0:T(2,128)(2,1)S(1)} async-done(((bf16[64,2,512]{2,1,0:T(2,128)(2,1)}), bf16[64,2,512]{2,1,0:T(2,128)(2,1)S(1)}, u32[]{:S(2)}, u32[]{:S(2)}) %all-to-all-start) | async-done | bytes 131104 | tf_op jit(solution)/shard_map/all_to_all | solution.py:62
  40.5 0.9 reshape.184
  41.4 6.4 %all-to-all-start.1 = ((bf16[8,2,4096]{2,1,0:T(2,128)(2,1)}), bf16[8,2,4096]{2,1,0:T(2,128)(2,1)S(1)}, u32[]{:S(2)}, u32[]{:S(2)}) async-start(bf16[8,2,4096]{2,1,0:T(2,128)(2,1)} %reshape.184), calls=%async_computation.1 | async-start | bytes 262144 | tf_op jit(solution)/shard_map/all_to_all | solution.py:64
  47.8 5.3 %all-to-all-done.1 = bf16[8,2,4096]{2,1,0:T(2,128)(2,1)S(1)} async-done(((bf16[8,2,4096]{2,1,0:T(2,128)(2,1)}), bf16[8,2,4096]{2,1,0:T(2,128)(2,1)S(1)}, u32[]{:S(2)}, u32[]{:S(2)}) %all-to-all-start.1) | async-done | bytes 131104 | tf_op jit(solution)/shard_map/all_to_all | solution.py:64
  53.6 0.6 gather_fusion.1
  54.2 0.6 gather_fusion.2
  54.9 0.9 %copy.61 = f32[32,16,64,2]{0,1,3,2:T(8,128)S(1)} copy(f32[32,16,64,2]{2,1,3,0:T(8,128)S(1)} %get-tuple-element.25) | data formatting | bytes 524288 | tf_op jit(solution)/shard_map/jit(_take)/select_n | solution.py:67
  55.9 1.0 %copy.62 = f32[32,1,16,64,2]{0,2,4,3,1:T(8,128)S(1)} copy(f32[32,1,16,64,2]{3,2,0,4,1:T(8,128)S(1)} %maximum_negate_fusion) | data formatting | bytes 524288 | tf_op jit(solution)/shard_map/neg | solution.py:69
  57.9 0.9 %copy.65 = f32[32,16,64,2]{0,1,3,2:T(8,128)S(1)} copy(f32[32,16,64,2]{2,1,3,0:T(8,128)S(1)} %get-tuple-element.24) | data formatting | bytes 524288 | tf_op jit(solution)/shard_map/jit(_take)/select_n | solution.py:66
  60.5 8.1 %all_to_all.20 = f32[8,1024,2]{1,2,0:T(2,128)S(1)} all-to-all(f32[8,1024,2]{1,2,0:T(2,128)S(1)} %copy.68), channel_id=1, replica_groups=mesh['chan'=8,'tm'=64] {'chan'}, dimensions={0} | all-to-all | bytes 131072 | tf_op jit(solution)/shard_map/all_to_all | solution.py:73
  69.1 0.9 reshape.186
  70.0 4.6 %all-to-all-start.3 = ((f32[64,1,256]{2,1,0:T(1,128)}), f32[64,1,256]{2,1,0:T(1,128)S(1)}, u32[]{:S(2)}, u32[]{:S(2)}) async-start(f32[64,1,256]{2,1,0:T(1,128)} %reshape.186), calls=%async_computation.3 | async-start | bytes 131072 | tf_op jit(solution)/shard_map/all_to_all | solution.py:75
  74.6 0.6 dynamic_slice.3
  75.2 0.6 compare_select_fusion.5
  75.9 9.9 %all-to-all-done.3 = f32[64,1,256]{2,1,0:T(1,128)S(1)} async-done(((f32[64,1,256]{2,1,0:T(1,128)}), f32[64,1,256]{2,1,0:T(1,128)S(1)}, u32[]{:S(2)}, u32[]{:S(2)}) %all-to-all-start.3) | async-done | bytes 65568 | tf_op jit(solution)/shard_map/all_to_all | solution.py:75
  86.3 0.8 reduce
  88.6 1.0 %convolution_bitcast_fusion = f32[16,2,8,256]{3,2,1,0:T(8,128)S(1)} fusion(f32[1024,256,1]{1,0,2:T(8,128)S(1)} %copy-done.1, f32[16,16,512]{2,1,0:T(8,128)S(1)} %get-tuple-element.21, f32[16,16,512]{2,1,0:T(8,128)S(1)} %get-tuple-element.20), kind=kOutput, calls=%fused_computation.17 | convolution fusion | flops 805568512 | bytes 2359296 | tf_op jit(solution)/shard_map/nrk,kl->rnl/dot_general | solution.py:51
  89.6 0.8 broadcast_multiply_fusion
  (60 shorter events, 6.8 us)
Async XLA Ops:
  0.0 1.8 %copy-start = (f32[512,512,1]{1,0,2:T(8,128)S(1)}, f32[512,512,1]{1,0,2:T(8,128)}, u32[]{:S(2)}) copy-start(f32[512,512,1]{1,0,2:T(8,128)} %constant.91) | copy-start | bytes 3145732
  1.9 3.4 %copy-start.7 = (f32[512,512,1]{1,0,2:T(8,128)S(1)}, f32[512,512,1]{1,0,2:T(8,128)}, u32[]{:S(2)}) copy-start(f32[512,512,1]{1,0,2:T(8,128)} %constant.92) | copy-start | bytes 3145732
  1.9 3.4 %copy-start.8 = (f32[12,512]{1,0:T(8,128)S(1)}, f32[12,512]{1,0:T(8,128)}, u32[]{:S(2)}) copy-start(f32[12,512]{1,0:T(8,128)} %constant.87) | copy-start | bytes 73732
  1.9 3.4 %copy-start.9 = (f32[12,512]{1,0:T(8,128)S(1)}, f32[12,512]{1,0:T(8,128)}, u32[]{:S(2)}) copy-start(f32[12,512]{1,0:T(8,128)} %constant.88) | copy-start | bytes 73732
  5.3 4.2 %copy-start.5 = (s32[64]{0:T(128)S(1)}, s32[64]{0:T(128)}, u32[]{:S(2)}) copy-start(s32[64]{0:T(128)} %param.14) | copy-start | bytes 772
  9.0 19.6 %copy-start.4 = (s32[32,2]{0,1:T(2,128)S(1)}, s32[32,2]{0,1:T(2,128)}, u32[]{:S(2)}) copy-start(s32[32,2]{0,1:T(2,128)} %param.15) | copy-start | bytes 772
  11.5 28.7 %all-to-all-start = ((bf16[64,2,512]{2,1,0:T(2,128)(2,1)}), bf16[64,2,512]{2,1,0:T(2,128)(2,1)S(1)}, u32[]{:S(2)}, u32[]{:S(2)}) async-start(bf16[64,2,512]{2,1,0:T(2,128)(2,1)} %reshape.182), calls=%async_computation | async-start | bytes 262144 | tf_op jit(solution)/shard_map/all_to_all | solution.py:62
  41.4 11.7 %all-to-all-start.1 = ((bf16[8,2,4096]{2,1,0:T(2,128)(2,1)}), bf16[8,2,4096]{2,1,0:T(2,128)(2,1)S(1)}, u32[]{:S(2)}, u32[]{:S(2)}) async-start(bf16[8,2,4096]{2,1,0:T(2,128)(2,1)} %reshape.184), calls=%async_computation.1 | async-start | bytes 262144 | tf_op jit(solution)/shard_map/all_to_all | solution.py:64
  60.1 14.5 %copy-start.6 = (s32[8]{0:T(128)S(1)}, s32[8]{0:T(128)}, u32[]{:S(2)}) copy-start(s32[8]{0:T(128)} %param.16) | copy-start | bytes 100
  70.0 15.8 %all-to-all-start.3 = ((f32[64,1,256]{2,1,0:T(1,128)}), f32[64,1,256]{2,1,0:T(1,128)S(1)}, u32[]{:S(2)}, u32[]{:S(2)}) async-start(f32[64,1,256]{2,1,0:T(1,128)} %reshape.186), calls=%async_computation.3 | async-start | bytes 131072 | tf_op jit(solution)/shard_map/all_to_all | solution.py:75
  87.1 0.8 copy-start.2
  87.1 0.8 copy-start.3
  87.3 1.2 %copy-start.1 = (f32[1024,256,1]{1,0,2:T(8,128)S(1)}, f32[1024,256,1]{1,0,2:T(8,128)}, u32[]{:S(2)}) copy-start(f32[1024,256,1]{1,0,2:T(8,128)} %constant.93) | copy-start | bytes 3145732

commit v2 on v1

v2 whole, which is shorter than its diff:
```python
import functools
import math

import jax
import jax.numpy as jnp
import numpy as np
from jax import lax
from jax.experimental import pallas as pl
from jax.experimental.pallas import tpu as pltpu
from jax.sharding import PartitionSpec as P

BLOCK = 16
SLOTS = 4
TRANSFORM_LENGTH = 16384
BAND_FIRST_BIN = 80
BINS = 512
LAGS = 4096
NEAR = 512
LAG_NEAR = 256
LANES = 128
MESH = pl.DeviceIdType.MESH
F32 = jnp.float32
BF16 = jnp.bfloat16


def phase(products):
    angles = np.mod(products, TRANSFORM_LENGTH) * (2.0 * math.pi / TRANSFORM_LENGTH)
    return np.cos(angles), np.sin(angles)


def split(table):
    table = table.astype(np.float32)
    high = table.astype(BF16)
    low = (table - high.astype(np.float32)).astype(BF16)
    return np.stack([high, low])


def forward_tables(samples):
    bins = BAND_FIRST_BIN + np.arange(BINS)
    cos, sin = phase(np.arange(NEAR)[:, None] * bins[None, :])
    tiles = BINS // LANES
    table = np.stack([cos.reshape(NEAR, tiles, LANES), -sin.reshape(NEAR, tiles, LANES)], axis=2)
    turn = phase(np.arange(samples // NEAR)[:, None] * NEAR * bins[None, :])
    return split(table.reshape(NEAR, 2 * BINS)), np.stack(turn).astype(np.float32)


def inverse_tables(scale):
    lane = np.arange(BINS)
    order = 8 * (lane % 64) + 4 * (lane // 64 % 2) + lane // 128
    bins = BAND_FIRST_BIN + order
    cos, sin = phase(bins[:, None] * np.arange(LAG_NEAR)[None, :])
    table = np.concatenate([cos, -sin], axis=0) * scale
    far = np.arange(LAGS // LAG_NEAR) * LAG_NEAR - LAGS // 2
    turn = phase(far[:, None] * bins[None, :])
    return split(table), np.stack(turn).astype(np.float32)


def halves(value):
    high = value.astype(BF16)
    return high, (value - high.astype(F32)).astype(BF16)


def zigzag(step):
    return 4 + (step + 1) // 2 * (1 - 2 * (step % 2))


def kernel(
    chans, windows,
    x_hbm, map_hbm, pairs_hbm, count_hbm, fwd_hbm, fturn_hbm, inv_hbm, iturn_hbm,
    out_ref,
    x_ref, map_ref, pairs_ref, count_ref, fwd_ref, fturn_ref, inv_ref, iturn_ref,
    high_ref, low_ref, z_ref, spec_ref,
    g_ref, r1_ref, s_ref, r2_ref, h_ref, sel_ref, pick_ref, m_ref, q_ref, m2_ref, u_ref, lag_h, lag_l,
    load_sem, send_sem, recv_sem,
):
    c, t = lax.axis_index("chan"), lax.axis_index("tm")
    rows, samples = x_ref.shape
    sections = samples // NEAR
    loads = [
        pltpu.make_async_copy(source, target, load_sem.at[k])
        for k, (source, target) in enumerate(
            (
                (x_hbm, x_ref), (fwd_hbm, fwd_ref), (fturn_hbm, fturn_ref), (map_hbm, map_ref),
                (pairs_hbm, pairs_ref), (count_hbm, count_ref), (inv_hbm, inv_ref), (iturn_hbm, iturn_ref),
            )
        )
    ]
    for load in loads:
        load.start()

    def window_peer(step):
        z = lax.rem(t // 8 + zigzag(step // 8), 8)
        y = lax.rem(lax.rem(t, 8) + zigzag(step % 8), 8)
        return z * 8 + y

    barrier = pltpu.get_barrier_semaphore()

    @pl.loop(0, windows - 1)
    def _(step):
        pl.semaphore_signal(barrier, 1, device_id=(c, window_peer(step)), device_id_type=MESH)

    @pl.loop(1, chans)
    def _(step):
        pl.semaphore_signal(barrier, 1, device_id=(lax.rem(c + step, chans), t), device_id_type=MESH)

    loads[0].wait()
    for b in range(sections):
        high, low = halves(x_ref[:, b * NEAR : (b + 1) * NEAR])
        high_ref[b * rows : (b + 1) * rows, :] = high
        low_ref[b * rows : (b + 1) * rows, :] = low
    loads[1].wait()
    loads[2].wait()

    for n in range(BINS // LANES):
        cols = slice(2 * LANES * n, 2 * LANES * (n + 1))
        z_ref[...] = (
            jnp.dot(high_ref[...], fwd_ref[0, :, cols], preferred_element_type=F32)
            + jnp.dot(low_ref[...], fwd_ref[0, :, cols], preferred_element_type=F32)
            + jnp.dot(high_ref[...], fwd_ref[1, :, cols], preferred_element_type=F32)
        )
        lanes = slice(LANES * n, LANES * (n + 1))
        re = jnp.zeros((rows, LANES), F32)
        im = jnp.zeros((rows, LANES), F32)
        for b in range(sections):
            zr = z_ref[b * rows : (b + 1) * rows, :LANES]
            zi = z_ref[b * rows : (b + 1) * rows, LANES:]
            cw = fturn_ref[0, b : b + 1, lanes]
            sw = fturn_ref[1, b : b + 1, lanes]
            re += zr * cw + zi * sw
            im += zi * cw - zr * sw
        spec_ref[:rows, lanes] = re
        spec_ref[rows:, lanes] = im

    re, im = spec_ref[:rows, :], spec_ref[rows:, :]
    power = re * re + im * im
    level = jnp.mean(power, axis=1, keepdims=True)
    inverse = 1.0 / jnp.sqrt(power + level + 1e-06)
    white = jnp.concatenate([re * inverse, im * inverse], axis=0).astype(BF16)

    loads[3].wait()
    place = jnp.bitwise_and(map_ref[...], rows - 1).reshape(1, rows)
    place = jnp.concatenate([place, place + rows], axis=1)
    pick = (lax.broadcasted_iota(jnp.int32, (2 * rows, 2 * rows), 0) == place).astype(F32).astype(BF16)
    g = lax.dot_general(white, pick, (((0,), (0,)), ((), ())), preferred_element_type=F32)
    g_ref[...] = g.reshape(windows, chans, 2 * rows)

    pl.semaphore_wait(barrier, windows + chans - 2)

    def send_window(source, target, k):
        def body(step, carry):
            peer = window_peer(step)
            pltpu.make_async_remote_copy(
                src_ref=source.at[peer], dst_ref=target.at[t], send_sem=send_sem.at[k],
                recv_sem=recv_sem.at[k], device_id=(c, peer), device_id_type=MESH,
            ).start()
            return carry

        lax.fori_loop(0, windows - 1, body, 0, unroll=7)
        target[t] = source[t]

    def arrived(target, k):
        part = target.at[pl.ds(0, target.shape[0] - 1)]
        pltpu.make_async_copy(part, part, recv_sem.at[k]).wait()

    def sent(source, k):
        part = source.at[pl.ds(0, source.shape[0] - 1)]
        pltpu.make_async_copy(part, part, send_sem.at[k]).wait()

    send_window(g_ref, r1_ref, 0)

    for load in loads[4:]:
        load.wait()
    pairs = pairs_ref.shape[1]
    gap = lax.broadcasted_iota(jnp.int32, (BLOCK, chans * rows), 1) - lax.broadcasted_iota(
        jnp.int32, (BLOCK, chans * rows), 0
    )
    for side in range(2):
        for p in range(pairs):
            hit = gap == pairs_ref[side, p] * BLOCK
            first = (side * pairs + p) * BLOCK
            sel_ref[first : first + BLOCK, :] = hit.astype(F32).astype(BF16)
    arrived(r1_ref, 0)
    for q in range(chans):
        s_ref[q] = r1_ref[:, q, :].astype(BF16)

    @pl.loop(1, chans)
    def _(step):
        peer = lax.rem(c + step, chans)
        pltpu.make_async_remote_copy(
            src_ref=s_ref.at[peer], dst_ref=r2_ref.at[c], send_sem=send_sem.at[1],
            recv_sem=recv_sem.at[1], device_id=(peer, t), device_id_type=MESH,
        ).start()

    r2_ref[c] = s_ref[c]
    arrived(r2_ref, 1)

    for d in range(chans):
        turned = r2_ref[d].astype(F32).T
        re, im = turned[:rows], turned[rows:]
        h_ref[d * rows : (d + 1) * rows, :] = jnp.concatenate([re, im, -im, re], axis=1).astype(BF16)
    pick_ref[...] = jnp.dot(sel_ref[...], h_ref[...], preferred_element_type=F32).astype(BF16)

    wide = SLOTS * BLOCK
    same = (
        lax.broadcasted_iota(jnp.int32, (wide, LANES), 0) // BLOCK
        == lax.broadcasted_iota(jnp.int32, (wide, LANES), 1) // (2 * BLOCK)
    )

    def owner_pairs(owner):
        first = pl.multiple_of(owner * wide, wide)
        left = pick_ref[pl.ds(first, wide), :LANES]
        both = pick_ref[pl.ds(pairs * BLOCK + first, wide), :]
        right = []
        for s in range(SLOTS):
            right += [both[s * BLOCK : (s + 1) * BLOCK, :LANES], both[s * BLOCK : (s + 1) * BLOCK, LANES:]]
        right = jnp.concatenate(right, axis=0)
        cross = lax.dot_general(left, right, (((1,), (1,)), ((), ())), preferred_element_type=F32)
        cross = jnp.where(same, cross, 0.0)
        return sum(cross[s * BLOCK : (s + 1) * BLOCK] for s in range(SLOTS))

    @pl.loop(1, chans)
    def _(step):
        owner = lax.rem(c + step, chans)
        m_ref[owner] = owner_pairs(owner)
        pltpu.make_async_remote_copy(
            src_ref=m_ref.at[owner], dst_ref=q_ref.at[c], send_sem=send_sem.at[2],
            recv_sem=recv_sem.at[2], device_id=(owner, t), device_id_type=MESH,
        ).start()

    q_ref[c] = owner_pairs(c)
    arrived(q_ref, 2)

    block = lax.broadcasted_iota(jnp.int32, (BLOCK, LANES), 1) // (2 * BLOCK)
    for s in range(SLOTS):
        for h in range(2):
            mixed = jnp.zeros((BLOCK, LANES), F32)
            for k in range(4):
                part = q_ref[4 * h + k]
                shift = (k - s) * 2 * BLOCK % LANES
                part = pltpu.roll(part, shift, 1) if shift else part
                mixed = jnp.where(block == k, part, mixed)
            m2_ref[s * BLOCK : (s + 1) * BLOCK, h, :] = mixed
    send_window(m2_ref, u_ref, 3)
    arrived(u_ref, 3)

    turned = jnp.concatenate([u_ref[:, 0, :], u_ref[:, 1, :]], axis=0).T
    row_ids = t * BLOCK + lax.broadcasted_iota(jnp.int32, (BLOCK, 1), 0)
    live = (row_ids < count_ref[c]).astype(F32)
    re = jnp.concatenate([turned[32 * k : 32 * k + 16] for k in range(4)], axis=1) * live
    im = jnp.concatenate([turned[32 * k + 16 : 32 * k + 32] for k in range(4)], axis=1) * live
    for n in range(LAGS // LAG_NEAR):
        cw, sw = iturn_ref[0, n : n + 1, :], iturn_ref[1, n : n + 1, :]
        place = slice(n * BLOCK, (n + 1) * BLOCK)
        high, low = halves(re * cw - im * sw)
        lag_h[place, :BINS] = high
        lag_l[place, :BINS] = low
        high, low = halves(re * sw + im * cw)
        lag_h[place, BINS:] = high
        lag_l[place, BINS:] = low
    lags = (
        jnp.dot(lag_h[...], inv_ref[0], preferred_element_type=F32)
        + jnp.dot(lag_l[...], inv_ref[0], preferred_element_type=F32)
        + jnp.dot(lag_h[...], inv_ref[1], preferred_element_type=F32)
    )
    for n in range(LAGS // LAG_NEAR):
        out_ref[:, n * LAG_NEAR : (n + 1) * LAG_NEAR] = lags[n * BLOCK : (n + 1) * BLOCK]
    sent(g_ref, 0)
    sent(s_ref, 1)
    sent(m_ref, 2)
    sent(m2_ref, 3)


def solution(mesh):
    chans, windows = mesh.shape["chan"], mesh.shape["tm"]

    def body(traces, channel_map, pair_blocks, pair_count):
        _, rows, samples = traces.shape
        fwd, fturn = forward_tables(samples)
        inv, iturn = inverse_tables(1.0 / math.sqrt(windows * BINS))
        sections, far = samples // NEAR, LAGS // LAG_NEAR
        vmem = pl.BlockSpec(memory_space=pltpu.VMEM)
        hbm = pl.BlockSpec(memory_space=pl.ANY)
        return pl.pallas_call(
            functools.partial(kernel, chans, windows),
            out_shape=jax.ShapeDtypeStruct((BLOCK, LAGS), F32),
            in_specs=[hbm] * 8,
            out_specs=vmem,
            scratch_shapes=[
                pltpu.VMEM((rows, samples), F32),
                pltpu.VMEM(channel_map.shape, jnp.int32),
                pltpu.SMEM(pair_blocks.shape[::-1], jnp.int32),
                pltpu.SMEM(pair_count.shape, jnp.int32),
                pltpu.VMEM(fwd.shape, BF16),
                pltpu.VMEM(fturn.shape, F32),
                pltpu.VMEM(inv.shape, BF16),
                pltpu.VMEM(iturn.shape, F32),
                pltpu.VMEM((sections * rows, NEAR), BF16),
                pltpu.VMEM((sections * rows, NEAR), BF16),
                pltpu.VMEM((sections * rows, 2 * LANES), F32),
                pltpu.VMEM((2 * rows, BINS), F32),
                pltpu.VMEM((windows, chans, 2 * rows), F32),
                pltpu.VMEM((windows, chans, 2 * rows), F32),
                pltpu.VMEM((chans, windows, 2 * rows), BF16),
                pltpu.VMEM((chans, windows, 2 * rows), BF16),
                pltpu.VMEM((chans * rows, 4 * windows), BF16),
                pltpu.VMEM((2 * pair_blocks.shape[0] * BLOCK, chans * rows), BF16),
                pltpu.VMEM((2 * pair_blocks.shape[0] * BLOCK, 4 * windows), BF16),
                pltpu.VMEM((chans, BLOCK, LANES), F32),
                pltpu.VMEM((chans, BLOCK, LANES), F32),
                pltpu.VMEM((windows, 2, LANES), F32),
                pltpu.VMEM((windows, 2, LANES), F32),
                pltpu.VMEM((far * BLOCK, 2 * BINS), BF16),
                pltpu.VMEM((far * BLOCK, 2 * BINS), BF16),
                pltpu.SemaphoreType.DMA((8,)),
                pltpu.SemaphoreType.DMA((4,)),
                pltpu.SemaphoreType.DMA((4,)),
            ],
            compiler_params=pltpu.CompilerParams(
                collective_id=0, has_side_effects=True, vmem_limit_bytes=63 << 20
            ),
            name="correlate",
        )(traces[0], channel_map, pair_blocks.T, pair_count, fwd, fturn, inv, iturn)

    placed = (P("tm", "chan", None), P("chan"), P(), P())
    return jax.shard_map(
        body, mesh=mesh, in_specs=placed, out_specs=P(("chan", "tm"), None), check_vma=False
    )
```

time: 90.8 us -> 46.5 us (0.51)
  Pallas kernels: 0 us -> 44.6 us
  starting transfers between devices: 28.2 us -> 0 us
  waiting for transfers between devices: 26.7 us -> 0 us
  local copies, waits for them, and re-layouts: 15.3 us -> 1.67 us
  matrix products: 8.7 us -> 0 us
  blocking collectives: 8.09 us -> 0 us
  other arithmetic: 2.97 us -> 0 us
    pallas_call x0 -> x1, Pallas kernels: none -> 44.6 us  [body(): pl.pallas_call(functools.partial(kernel, chans, windows), out_shape=jax.S...]
    all_to_all x3 -> x0, starting transfers between devices: 28.2 us -> none  [the longest x1 17.1 us: body(): fibre = lax.all_to_all(fibre, 'tm', 0, 0, tiled=True)]
    all_to_all x3 -> x0, waiting for transfers between devices: 26.7 us -> none  [the longest x1 11.5 us: body(): fibre = lax.all_to_all(fibre, 'tm', 0, 0, tiled=True)]
    dot_general x4 -> x0, matrix products: 8.7 us -> none  [the longest x1 3.75 us: forward_spectrum(): im = jnp.einsum('cba,ak->bck', parts, -sin_t, precision=HIGHEST)]
    all_to_all x1 -> x0, blocking collectives: 8.09 us -> none  [body(): stacked = lax.all_to_all(stacked, 'chan', 0, 0, tiled=True)]
    another operation x3 -> x0, local copies, waits for them, and re-layouts: 2.45 us -> none  [the longest x1 1.83 us: forward_spectrum(): parts = window.reshape(rows, samples // FIRST, FIRST)]
    unnamed x26 -> x1, local copies, waits for them, and re-layouts: 4.1 us -> 1.67 us
    gather x4 -> x0, local copies, waits for them, and re-layouts: 2.2 us -> none  [the longest x2 1.03 us: body(): fibre = jnp.take(fibre, jnp.mod(channel_map, chan_dev), axis=1)]
  transfers between devices with their start and end apart: 3 -> 0, of which waited for: 3 -> 0; matrix products, arithmetic and copies ran while one was open for 1% -> 0% of each run, Pallas kernels for 0% -> 0%
where the time goes in v2:
time: 46.5 us; the launch traced here: 46.3 us
  Pallas kernels  44.6 us (96%)
  local copies, waits for them, and re-layouts  1.67 us (4%)
    pallas_call x1, Pallas kernels, body(): pl.pallas_call(functools.partial(kernel, chans, windows), out_shape=jax.S...  44.6 us
    unnamed x1, local copies, waits for them, and re-layouts  1.67 us

profile of v2, /device:TPU:1, one launch (start us, length us, event | category | flops | bytes accessed | tf_op | source)
XLA Modules:
  0.0 46.3 jit_solution(12556618728984612025)
XLA Ops:
  0.0 44.6 %correlate.1 = f32[16,4096]{1,0:T(8,128)} custom-call(f32[64,6144]{1,0:T(8,128)} %bitcast.2, s32[64]{0:T(128)} %map_hbm.1, s32[2,32]{1,0:T(2,128)} %bitcast.3, s32[8]{0:T(128)} %count_hbm.1, bf16[2,512,1024]{2,1,0:T(8,128)(2,1)} %constant.8.clone.fwd_hbm, f32[2,12,512]{2,1,0:T(8,128)} %constant.9.clone.fturn_hbm, ...), custom_call_target="tpu_custom_call" | custom-call | tf_op jit(solution)/shard_map/correlate/pallas_call | solution.py:283
  44.6 1.7 %copy.10 = f32[16,4096]{1,0:T(8,128)} copy(f32[16,4096]{1,0:T(8,128)} %correlate.1) | data formatting | bytes 524288

commit v3 on v2

--- a/solution.py
+++ b/solution.py
@@ -16,15 +16,15 @@
 BINS = 512
 LAGS = 4096
 NEAR = 512
-LAG_NEAR = 256
+LAG_NEAR = 512
 LANES = 128
 MESH = pl.DeviceIdType.MESH
 F32 = jnp.float32
 BF16 = jnp.bfloat16
 
 
-def phase(products):
-    angles = np.mod(products, TRANSFORM_LENGTH) * (2.0 * math.pi / TRANSFORM_LENGTH)
+def phase(products, length=TRANSFORM_LENGTH):
+    angles = np.mod(products, length) * (2.0 * math.pi / length)
     return np.cos(angles), np.sin(angles)
 
 
@@ -37,11 +37,11 @@
 
 def forward_tables(samples):
     bins = BAND_FIRST_BIN + np.arange(BINS)
-    cos, sin = phase(np.arange(NEAR)[:, None] * bins[None, :])
-    tiles = BINS // LANES
-    table = np.stack([cos.reshape(NEAR, tiles, LANES), -sin.reshape(NEAR, tiles, LANES)], axis=2)
-    turn = phase(np.arange(samples // NEAR)[:, None] * NEAR * bins[None, :])
-    return split(table.reshape(NEAR, 2 * BINS)), np.stack(turn).astype(np.float32)
+    offset = 2 * np.arange(NEAR // 2) + 1
+    cos, sin = phase(offset[:, None] * bins[None, :], 2 * TRANSFORM_LENGTH)
+    centre = 2 * NEAR * np.arange(samples // NEAR) + NEAR - 1
+    turn = phase(centre[:, None] * bins[None, :], 2 * TRANSFORM_LENGTH)
+    return split(np.stack([cos, -sin])), np.stack(turn).astype(np.float32)
 
 
 def inverse_tables(scale):
@@ -69,25 +69,20 @@
     x_hbm, map_hbm, pairs_hbm, count_hbm, fwd_hbm, fturn_hbm, inv_hbm, iturn_hbm,
     out_ref,
     x_ref, map_ref, pairs_ref, count_ref, fwd_ref, fturn_ref, inv_ref, iturn_ref,
-    high_ref, low_ref, z_ref, spec_ref,
-    g_ref, r1_ref, s_ref, r2_ref, h_ref, sel_ref, pick_ref, m_ref, q_ref, m2_ref, u_ref, lag_h, lag_l,
+    even_h, even_l, odd_h, odd_l, zr_ref, zi_ref, spec_ref,
+    g_ref, r1_ref, wide_ref, s_ref, r2_ref, h_ref, sel_ref, m_ref, q_ref, m2_ref, u_ref, lag_h, lag_l,
     load_sem, send_sem, recv_sem,
 ):
     c, t = lax.axis_index("chan"), lax.axis_index("tm")
     rows, samples = x_ref.shape
     sections = samples // NEAR
+    ends = [
+        (x_hbm, x_ref), (fwd_hbm, fwd_ref), (fturn_hbm, fturn_ref), (map_hbm, map_ref),
+        (pairs_hbm, pairs_ref), (count_hbm, count_ref), (iturn_hbm, iturn_ref), (inv_hbm, inv_ref),
+    ]
     loads = [
-        pltpu.make_async_copy(source, target, load_sem.at[k])
-        for k, (source, target) in enumerate(
-            (
-                (x_hbm, x_ref), (fwd_hbm, fwd_ref), (fturn_hbm, fturn_ref), (map_hbm, map_ref),
-                (pairs_hbm, pairs_ref), (count_hbm, count_ref), (inv_hbm, inv_ref), (iturn_hbm, iturn_ref),
-            )
-        )
+        pltpu.make_async_copy(source, target, load_sem.at[k]) for k, (source, target) in enumerate(ends)
     ]
-    for load in loads:
-        load.start()
-
     def window_peer(step):
         z = lax.rem(t // 8 + zigzag(step // 8), 8)
         y = lax.rem(lax.rem(t, 8) + zigzag(step % 8), 8)
@@ -95,35 +90,56 @@
 
     barrier = pltpu.get_barrier_semaphore()
 
-    @pl.loop(0, windows - 1)
-    def _(step):
+    def greet(step):
         pl.semaphore_signal(barrier, 1, device_id=(c, window_peer(step)), device_id_type=MESH)
+
+    pl.loop(0, windows // 2)(greet)
+    for load in loads[:6]:
+        load.start()
+    pl.loop(windows // 2, windows - 1)(greet)
 
     @pl.loop(1, chans)
     def _(step):
         pl.semaphore_signal(barrier, 1, device_id=(lax.rem(c + step, chans), t), device_id_type=MESH)
 
+    half = NEAR // 2
+    mirror = (
+        lax.broadcasted_iota(jnp.int32, (half, half), 0) + lax.broadcasted_iota(jnp.int32, (half, half), 1)
+        == half - 1
+    ).astype(F32).astype(BF16)
     loads[0].wait()
     for b in range(sections):
-        high, low = halves(x_ref[:, b * NEAR : (b + 1) * NEAR])
-        high_ref[b * rows : (b + 1) * rows, :] = high
-        low_ref[b * rows : (b + 1) * rows, :] = low
+        place = slice(b * rows, (b + 1) * rows)
+        even_h[place, :], even_l[place, :] = halves(x_ref[:, b * NEAR : b * NEAR + half])
+    back = jnp.dot(even_h[...], mirror, preferred_element_type=F32) + jnp.dot(
+        even_l[...], mirror, preferred_element_type=F32
+    )
+    for b in range(sections):
+        place = slice(b * rows, (b + 1) * rows)
+        ahead = x_ref[:, b * NEAR + half : (b + 1) * NEAR]
+        even_h[place, :], even_l[place, :] = halves(ahead + back[place])
+        odd_h[place, :], odd_l[place, :] = halves(ahead - back[place])
     loads[1].wait()
     loads[2].wait()
-
-    for n in range(BINS // LANES):
-        cols = slice(2 * LANES * n, 2 * LANES * (n + 1))
-        z_ref[...] = (
-            jnp.dot(high_ref[...], fwd_ref[0, :, cols], preferred_element_type=F32)
-            + jnp.dot(low_ref[...], fwd_ref[0, :, cols], preferred_element_type=F32)
-            + jnp.dot(high_ref[...], fwd_ref[1, :, cols], preferred_element_type=F32)
+    for load in loads[6:]:
+        load.start()
+
+    def product(high, low, part, lanes):
+        return (
+            jnp.dot(high[...], fwd_ref[0, part, :, lanes], preferred_element_type=F32)
+            + jnp.dot(low[...], fwd_ref[0, part, :, lanes], preferred_element_type=F32)
+            + jnp.dot(high[...], fwd_ref[1, part, :, lanes], preferred_element_type=F32)
         )
-        lanes = slice(LANES * n, LANES * (n + 1))
-        re = jnp.zeros((rows, LANES), F32)
-        im = jnp.zeros((rows, LANES), F32)
+
+    for n in range(BINS // half):
+        lanes = slice(half * n, half * (n + 1))
+        zr_ref[...] = product(even_h, even_l, 0, lanes)
+        zi_ref[...] = product(odd_h, odd_l, 1, lanes)
+        re = jnp.zeros((rows, half), F32)
+        im = jnp.zeros((rows, half), F32)
         for b in range(sections):
-            zr = z_ref[b * rows : (b + 1) * rows, :LANES]
-            zi = z_ref[b * rows : (b + 1) * rows, LANES:]
+            zr = zr_ref[b * rows : (b + 1) * rows, :]
+            zi = zi_ref[b * rows : (b + 1) * rows, :]
             cw = fturn_ref[0, b : b + 1, lanes]
             sw = fturn_ref[1, b : b + 1, lanes]
             re += zr * cw + zi * sw
@@ -142,7 +158,7 @@
     place = jnp.concatenate([place, place + rows], axis=1)
     pick = (lax.broadcasted_iota(jnp.int32, (2 * rows, 2 * rows), 0) == place).astype(F32).astype(BF16)
     g = lax.dot_general(white, pick, (((0,), (0,)), ((), ())), preferred_element_type=F32)
-    g_ref[...] = g.reshape(windows, chans, 2 * rows)
+    g_ref[...] = g.reshape(windows, chans, 2 * rows).astype(BF16)
 
     pl.semaphore_wait(barrier, windows + chans - 2)
 
@@ -158,34 +174,37 @@
         lax.fori_loop(0, windows - 1, body, 0, unroll=7)
         target[t] = source[t]
 
-    def arrived(target, k):
-        part = target.at[pl.ds(0, target.shape[0] - 1)]
-        pltpu.make_async_copy(part, part, recv_sem.at[k]).wait()
-
-    def sent(source, k):
-        part = source.at[pl.ds(0, source.shape[0] - 1)]
-        pltpu.make_async_copy(part, part, send_sem.at[k]).wait()
+    def arrived(ref, k):
+        rest = ref.at[pl.ds(0, ref.shape[0] - 1)]
+        pltpu.make_async_copy(rest, rest, recv_sem.at[k]).wait()
+
+    def sent(ref, k):
+        rest = ref.at[pl.ds(0, ref.shape[0] - 1)]
+        pltpu.make_async_copy(rest, rest, send_sem.at[k]).wait()
 
     send_window(g_ref, r1_ref, 0)
 
     for load in loads[4:]:
         load.wait()
-    pairs = pairs_ref.shape[1]
     gap = lax.broadcasted_iota(jnp.int32, (BLOCK, chans * rows), 1) - lax.broadcasted_iota(
         jnp.int32, (BLOCK, chans * rows), 0
     )
-    for side in range(2):
-        for p in range(pairs):
-            hit = gap == pairs_ref[side, p] * BLOCK
-            first = (side * pairs + p) * BLOCK
-            sel_ref[first : first + BLOCK, :] = hit.astype(F32).astype(BF16)
+    wide = SLOTS * BLOCK
+    owners = [lax.rem(c + zigzag(step) % chans, chans) for step in range(chans)]
+    for step in range(chans):
+        for side in range(2):
+            for s in range(SLOTS):
+                hit = gap == pairs_ref[side, owners[step] * SLOTS + s] * BLOCK
+                first = (step * 2 + side) * wide + s * BLOCK
+                sel_ref[first : first + BLOCK, :] = hit.astype(F32).astype(BF16)
     arrived(r1_ref, 0)
+    wide_ref[...] = r1_ref[...].astype(F32)
     for q in range(chans):
-        s_ref[q] = r1_ref[:, q, :].astype(BF16)
-
-    @pl.loop(1, chans)
+        s_ref[q] = wide_ref[:, q, :].astype(BF16)
+
+    @pl.loop(0, chans - 1)
     def _(step):
-        peer = lax.rem(c + step, chans)
+        peer = lax.rem(c + zigzag(step), chans)
         pltpu.make_async_remote_copy(
             src_ref=s_ref.at[peer], dst_ref=r2_ref.at[c], send_sem=send_sem.at[1],
             recv_sem=recv_sem.at[1], device_id=(peer, t), device_id_type=MESH,
@@ -194,22 +213,26 @@
     r2_ref[c] = s_ref[c]
     arrived(r2_ref, 1)
 
-    for d in range(chans):
-        turned = r2_ref[d].astype(F32).T
-        re, im = turned[:rows], turned[rows:]
-        h_ref[d * rows : (d + 1) * rows, :] = jnp.concatenate([re, im, -im, re], axis=1).astype(BF16)
-    pick_ref[...] = jnp.dot(sel_ref[...], h_ref[...], preferred_element_type=F32).astype(BF16)
-
-    wide = SLOTS * BLOCK
+    for d in range(0, chans, 2):
+        one = r2_ref[d].astype(F32)
+        two = r2_ref[d + 1].astype(F32)
+        first = lax.broadcasted_iota(jnp.int32, one.shape, 1) < rows
+        re = jnp.where(first, one, pltpu.roll(two, rows, 1))
+        im = jnp.where(first, pltpu.roll(one, rows, 1), two)
+        value = jnp.concatenate([re, im, -im, re], axis=0)
+        h_ref[:, d * rows : (d + 2) * rows] = value.astype(BF16)
+    pick = lax.dot_general(
+        sel_ref[...], h_ref[...], (((1,), (1,)), ((), ())), preferred_element_type=F32
+    ).astype(BF16)
+
     same = (
         lax.broadcasted_iota(jnp.int32, (wide, LANES), 0) // BLOCK
         == lax.broadcasted_iota(jnp.int32, (wide, LANES), 1) // (2 * BLOCK)
     )
 
-    def owner_pairs(owner):
-        first = pl.multiple_of(owner * wide, wide)
-        left = pick_ref[pl.ds(first, wide), :LANES]
-        both = pick_ref[pl.ds(pairs * BLOCK + first, wide), :]
+    def owner_pairs(step):
+        left = pick[2 * step * wide : (2 * step + 1) * wide, :LANES]
+        both = pick[(2 * step + 1) * wide : (2 * step + 2) * wide]
         right = []
         for s in range(SLOTS):
             right += [both[s * BLOCK : (s + 1) * BLOCK, :LANES], both[s * BLOCK : (s + 1) * BLOCK, LANES:]]
@@ -218,16 +241,13 @@
         cross = jnp.where(same, cross, 0.0)
         return sum(cross[s * BLOCK : (s + 1) * BLOCK] for s in range(SLOTS))
 
-    @pl.loop(1, chans)
-    def _(step):
-        owner = lax.rem(c + step, chans)
-        m_ref[owner] = owner_pairs(owner)
+    for step in range(chans - 1):
+        m_ref[step] = owner_pairs(step)
         pltpu.make_async_remote_copy(
-            src_ref=m_ref.at[owner], dst_ref=q_ref.at[c], send_sem=send_sem.at[2],
-            recv_sem=recv_sem.at[2], device_id=(owner, t), device_id_type=MESH,
+            src_ref=m_ref.at[step], dst_ref=q_ref.at[c], send_sem=send_sem.at[2],
+            recv_sem=recv_sem.at[2], device_id=(owners[step], t), device_id_type=MESH,
         ).start()
-
-    q_ref[c] = owner_pairs(c)
+    q_ref[c] = owner_pairs(chans - 1)
     arrived(q_ref, 2)
 
     block = lax.broadcasted_iota(jnp.int32, (BLOCK, LANES), 1) // (2 * BLOCK)
@@ -279,10 +299,10 @@
         inv, iturn = inverse_tables(1.0 / math.sqrt(windows * BINS))
         sections, far = samples // NEAR, LAGS // LAG_NEAR
         vmem = pl.BlockSpec(memory_space=pltpu.VMEM)
-        hbm = pl.BlockSpec(memory_space=pl.ANY)
+        hbm = pl.BlockSpec(memory_space=pltpu.HBM)
         return pl.pallas_call(
             functools.partial(kernel, chans, windows),
-            out_shape=jax.ShapeDtypeStruct((BLOCK, LAGS), F32),
+            out_shape=pltpu.VMEM((BLOCK, LAGS), F32),
             in_specs=[hbm] * 8,
             out_specs=vmem,
             scratch_shapes=[
@@ -294,17 +314,20 @@
                 pltpu.VMEM(fturn.shape, F32),
                 pltpu.VMEM(inv.shape, BF16),
                 pltpu.VMEM(iturn.shape, F32),
-                pltpu.VMEM((sections * rows, NEAR), BF16),
-                pltpu.VMEM((sections * rows, NEAR), BF16),
-                pltpu.VMEM((sections * rows, 2 * LANES), F32),
+                pltpu.VMEM((sections * rows, NEAR // 2), BF16),
+                pltpu.VMEM((sections * rows, NEAR // 2), BF16),
+                pltpu.VMEM((sections * rows, NEAR // 2), BF16),
+                pltpu.VMEM((sections * rows, NEAR // 2), BF16),
+                pltpu.VMEM((sections * rows, NEAR // 2), F32),
+                pltpu.VMEM((sections * rows, NEAR // 2), F32),
                 pltpu.VMEM((2 * rows, BINS), F32),
-                pltpu.VMEM((windows, chans, 2 * rows), F32),
+                pltpu.VMEM((windows, chans, 2 * rows), BF16),
+                pltpu.VMEM((windows, chans, 2 * rows), BF16),
                 pltpu.VMEM((windows, chans, 2 * rows), F32),
                 pltpu.VMEM((chans, windows, 2 * rows), BF16),
                 pltpu.VMEM((chans, windows, 2 * rows), BF16),
-                pltpu.VMEM((chans * rows, 4 * windows), BF16),
+                pltpu.VMEM((4 * windows, chans * rows), BF16),
                 pltpu.VMEM((2 * pair_blocks.shape[0] * BLOCK, chans * rows), BF16),
-                pltpu.VMEM((2 * pair_blocks.shape[0] * BLOCK, 4 * windows), BF16),
                 pltpu.VMEM((chans, BLOCK, LANES), F32),
                 pltpu.VMEM((chans, BLOCK, LANES), F32),
                 pltpu.VMEM((windows, 2, LANES), F32),
@@ -316,7 +339,7 @@
                 pltpu.SemaphoreType.DMA((4,)),
             ],
             compiler_params=pltpu.CompilerParams(
-                collective_id=0, has_side_effects=True, vmem_limit_bytes=63 << 20
+                collective_id=0, has_side_effects=True, vmem_limit_bytes=56 << 20
             ),
             name="correlate",
         )(traces[0], channel_map, pair_blocks.T, pair_count, fwd, fturn, inv, iturn)

time: 46.5 us -> 41.8 us (0.90)
  Pallas kernels: 44.6 us -> 41 us
  local copies, waits for them, and re-layouts: 1.67 us -> 0.71 us
    pallas_call x1, Pallas kernels: 44.6 us -> 41 us  [body(): pl.pallas_call(functools.partial(kernel, chans, windows), out_shape=pltpu...]
    unnamed x1, local copies, waits for them, and re-layouts: 1.67 us -> 0.71 us
where the time goes in v3:
time: 41.8 us; the launch traced here: 41.7 us
  Pallas kernels  41 us (98%)
  local copies, waits for them, and re-layouts  0.71 us (2%)
    pallas_call x1, Pallas kernels, body(): pl.pallas_call(functools.partial(kernel, chans, windows), out_shape=pltpu...  41 us

profile of v3, /device:TPU:1, one launch (start us, length us, event | category | flops | bytes accessed | tf_op | source)
XLA Modules:
  0.0 41.7 jit_solution(13484095944983274680)
XLA Ops:
  0.0 41.0 %correlate.1 = f32[16,4096]{1,0:T(8,128)S(1)} custom-call(f32[64,6144]{1,0:T(8,128)} %bitcast.2, s32[64]{0:T(128)} %map_hbm.1, s32[2,32]{1,0:T(2,128)} %bitcast.3, s32[8]{0:T(128)} %count_hbm.1, bf16[2,2,256,512]{3,2,1,0:T(8,128)(2,1)} %constant.8.clone.fwd_hbm, f32[2,12,512]{2,1,0:T(8,128)} %constant.9.clone.fturn_hbm, ...), custom_call_target="tpu_custom_call" | custom-call | tf_op jit(solution)/shard_map/correlate/pallas_call | solution.py:303
  41.0 0.7 %copy.10 = f32[16,4096]{1,0:T(8,128)} copy(f32[16,4096]{1,0:T(8,128)S(1)} %correlate.1) | data formatting | bytes 524288

commit v4 on v3

--- a/solution.py
+++ b/solution.py
@@ -84,19 +84,26 @@
         pltpu.make_async_copy(source, target, load_sem.at[k]) for k, (source, target) in enumerate(ends)
     ]
     def window_peer(step):
-        z = lax.rem(t // 8 + zigzag(step // 8), 8)
-        y = lax.rem(lax.rem(t, 8) + zigzag(step % 8), 8)
+        z = lax.rem(t // 8 + zigzag(step[0]), 8)
+        y = lax.rem(lax.rem(t, 8) + zigzag(step[1]), 8)
         return z * 8 + y
+
+    def diagonal(total, action):
+        @pl.loop(max(0, total - 7), min(7, total) + 1)
+        def _(i):
+            action((i, total - i))
 
     barrier = pltpu.get_barrier_semaphore()
 
     def greet(step):
         pl.semaphore_signal(barrier, 1, device_id=(c, window_peer(step)), device_id_type=MESH)
 
-    pl.loop(0, windows // 2)(greet)
+    for total in range(7):
+        diagonal(total, greet)
     for load in loads[:6]:
         load.start()
-    pl.loop(windows // 2, windows - 1)(greet)
+    for total in range(7, 14):
+        diagonal(total, greet)
 
     @pl.loop(1, chans)
     def _(step):
@@ -163,15 +170,15 @@
     pl.semaphore_wait(barrier, windows + chans - 2)
 
     def send_window(source, target, k):
-        def body(step, carry):
+        def action(step):
             peer = window_peer(step)
             pltpu.make_async_remote_copy(
                 src_ref=source.at[peer], dst_ref=target.at[t], send_sem=send_sem.at[k],
                 recv_sem=recv_sem.at[k], device_id=(c, peer), device_id_type=MESH,
             ).start()
-            return carry
-
-        lax.fori_loop(0, windows - 1, body, 0, unroll=7)
+
+        for total in range(14):
+            diagonal(total, action)
         target[t] = source[t]
 
     def arrived(ref, k):

time: 41.8 us -> 40.9 us (0.978)
  Pallas kernels: 41 us -> 40 us
    pallas_call x1, Pallas kernels: 41 us -> 40 us  [body(): pl.pallas_call(functools.partial(kernel, chans, windows), out_shape=pltpu...]
where the time goes in v4:
time: 40.9 us; the launch traced here: 40.8 us
  Pallas kernels  40 us (98%)
  local copies, waits for them, and re-layouts  0.71 us (2%)
    pallas_call x1, Pallas kernels, body(): pl.pallas_call(functools.partial(kernel, chans, windows), out_shape=pltpu...  40 us

profile of v4, /device:TPU:1, one launch (start us, length us, event | category | flops | bytes accessed | tf_op | source)
XLA Modules:
  0.0 40.8 jit_solution(15071487440170808705)
XLA Ops:
  0.0 40.0 %correlate.1 = f32[16,4096]{1,0:T(8,128)S(1)} custom-call(f32[64,6144]{1,0:T(8,128)} %bitcast.2, s32[64]{0:T(128)} %map_hbm.1, s32[2,32]{1,0:T(2,128)} %bitcast.3, s32[8]{0:T(128)} %count_hbm.1, bf16[2,2,256,512]{3,2,1,0:T(8,128)(2,1)} %constant.8.clone.fwd_hbm, f32[2,12,512]{2,1,0:T(8,128)} %constant.9.clone.fturn_hbm, ...), custom_call_target="tpu_custom_call" | custom-call | tf_op jit(solution)/shard_map/correlate/pallas_call | solution.py:310
  40.0 0.7 %copy.10 = f32[16,4096]{1,0:T(8,128)} copy(f32[16,4096]{1,0:T(8,128)S(1)} %correlate.1) | data formatting | bytes 524288

commit v5 on v4

--- a/solution.py
+++ b/solution.py
@@ -89,8 +89,7 @@
         return z * 8 + y
 
     def diagonal(total, action):
-        @pl.loop(max(0, total - 7), min(7, total) + 1)
-        def _(i):
+        for i in range(max(0, total - 7), min(7, total) + 1):
             action((i, total - i))
 
     barrier = pltpu.get_barrier_semaphore()
@@ -209,7 +208,7 @@
     for q in range(chans):
         s_ref[q] = wide_ref[:, q, :].astype(BF16)
 
-    @pl.loop(0, chans - 1)
+    @pl.loop(0, chans - 1, unroll=True)
     def _(step):
         peer = lax.rem(c + zigzag(step), chans)
         pltpu.make_async_remote_copy(

time: 40.9 us -> 40.7 us (level)
  no operation moved by 1% of the time
where the time goes in v5:
time: 40.7 us; the launch traced here: 40.6 us
  Pallas kernels  39.8 us (98%)
  local copies, waits for them, and re-layouts  0.71 us (2%)
    pallas_call x1, Pallas kernels, body(): pl.pallas_call(functools.partial(kernel, chans, windows), out_shape=pltpu...  39.8 us

profile of v5, /device:TPU:1, one launch (start us, length us, event | category | flops | bytes accessed | tf_op | source)
XLA Modules:
  0.0 40.6 jit_solution(10915697997933800247)
XLA Ops:
  0.0 39.8 %correlate.1 = f32[16,4096]{1,0:T(8,128)S(1)} custom-call(f32[64,6144]{1,0:T(8,128)} %bitcast.2, s32[64]{0:T(128)} %map_hbm.1, s32[2,32]{1,0:T(2,128)} %bitcast.3, s32[8]{0:T(128)} %count_hbm.1, bf16[2,2,256,512]{3,2,1,0:T(8,128)(2,1)} %constant.8.clone.fwd_hbm, f32[2,12,512]{2,1,0:T(8,128)} %constant.9.clone.fturn_hbm, ...), custom_call_target="tpu_custom_call" | custom-call | tf_op jit(solution)/shard_map/correlate/pallas_call | solution.py:309
  39.8 0.7 %copy.10 = f32[16,4096]{1,0:T(8,128)} copy(f32[16,4096]{1,0:T(8,128)S(1)} %correlate.1) | data formatting | bytes 524288

commit v6 on v5

--- a/solution.py
+++ b/solution.py
@@ -70,7 +70,7 @@
     out_ref,
     x_ref, map_ref, pairs_ref, count_ref, fwd_ref, fturn_ref, inv_ref, iturn_ref,
     even_h, even_l, odd_h, odd_l, zr_ref, zi_ref, spec_ref,
-    g_ref, r1_ref, wide_ref, s_ref, r2_ref, h_ref, sel_ref, m_ref, q_ref, m2_ref, u_ref, lag_h, lag_l,
+    g_ref, r1_ref, wide_ref, s_ref, r2_ref, h_ref, sel_ref, m_ref, q_ref, m2_ref, u_ref, lag_ref,
     load_sem, send_sem, recv_sem,
 ):
     c, t = lax.axis_index("chan"), lax.axis_index("tm")
@@ -274,20 +274,14 @@
     live = (row_ids < count_ref[c]).astype(F32)
     re = jnp.concatenate([turned[32 * k : 32 * k + 16] for k in range(4)], axis=1) * live
     im = jnp.concatenate([turned[32 * k + 16 : 32 * k + 32] for k in range(4)], axis=1) * live
+    depth = LAGS // LAG_NEAR * BLOCK
     for n in range(LAGS // LAG_NEAR):
         cw, sw = iturn_ref[0, n : n + 1, :], iturn_ref[1, n : n + 1, :]
-        place = slice(n * BLOCK, (n + 1) * BLOCK)
-        high, low = halves(re * cw - im * sw)
-        lag_h[place, :BINS] = high
-        lag_l[place, :BINS] = low
-        high, low = halves(re * sw + im * cw)
-        lag_h[place, BINS:] = high
-        lag_l[place, BINS:] = low
-    lags = (
-        jnp.dot(lag_h[...], inv_ref[0], preferred_element_type=F32)
-        + jnp.dot(lag_l[...], inv_ref[0], preferred_element_type=F32)
-        + jnp.dot(lag_h[...], inv_ref[1], preferred_element_type=F32)
-    )
+        place, lower = slice(n * BLOCK, (n + 1) * BLOCK), slice(depth + n * BLOCK, depth + (n + 1) * BLOCK)
+        lag_ref[place, :BINS], lag_ref[lower, :BINS] = halves(re * cw - im * sw)
+        lag_ref[place, BINS:], lag_ref[lower, BINS:] = halves(re * sw + im * cw)
+    both = jnp.dot(lag_ref[...], inv_ref[0], preferred_element_type=F32)
+    lags = both[:depth] + both[depth:] + jnp.dot(lag_ref[:depth], inv_ref[1], preferred_element_type=F32)
     for n in range(LAGS // LAG_NEAR):
         out_ref[:, n * LAG_NEAR : (n + 1) * LAG_NEAR] = lags[n * BLOCK : (n + 1) * BLOCK]
     sent(g_ref, 0)
@@ -338,8 +332,7 @@
                 pltpu.VMEM((chans, BLOCK, LANES), F32),
                 pltpu.VMEM((windows, 2, LANES), F32),
                 pltpu.VMEM((windows, 2, LANES), F32),
-                pltpu.VMEM((far * BLOCK, 2 * BINS), BF16),
-                pltpu.VMEM((far * BLOCK, 2 * BINS), BF16),
+                pltpu.VMEM((2 * far * BLOCK, 2 * BINS), BF16),
                 pltpu.SemaphoreType.DMA((8,)),
                 pltpu.SemaphoreType.DMA((4,)),
                 pltpu.SemaphoreType.DMA((4,)),

time: 40.7 us -> 40.7 us (level)
  no operation moved by 1% of the time
where the time goes in v6:
time: 40.7 us; the launch traced here: 40.5 us
  Pallas kernels  39.8 us (98%)
  local copies, waits for them, and re-layouts  0.71 us (2%)
    pallas_call x1, Pallas kernels, body(): pl.pallas_call(functools.partial(kernel, chans, windows), out_shape=pltpu...  39.8 us

profile of v6, /device:TPU:1, one launch (start us, length us, event | category | flops | bytes accessed | tf_op | source)
XLA Modules:
  0.0 40.5 jit_solution(6630811269378773645)
XLA Ops:
  0.0 39.8 %correlate.1 = f32[16,4096]{1,0:T(8,128)S(1)} custom-call(f32[64,6144]{1,0:T(8,128)} %bitcast.2, s32[64]{0:T(128)} %map_hbm.1, s32[2,32]{1,0:T(2,128)} %bitcast.3, s32[8]{0:T(128)} %count_hbm.1, bf16[2,2,256,512]{3,2,1,0:T(8,128)(2,1)} %constant.8.clone.fwd_hbm, f32[2,12,512]{2,1,0:T(8,128)} %constant.9.clone.fturn_hbm, ...), custom_call_target="tpu_custom_call" | custom-call | tf_op jit(solution)/shard_map/correlate/pallas_call | solution.py:303
  39.8 0.7 %copy.10 = f32[16,4096]{1,0:T(8,128)} copy(f32[16,4096]{1,0:T(8,128)S(1)} %correlate.1) | data formatting | bytes 524288
